TPU v7x, 32 devices: a whole 2x2x4 slice. The times are simulated.
32 devices in a mesh: seq: 8 (over y, x, core), ch: 4 (over z).
Axes of the slice: x: 2, y: 2, z: 4, core: 2. Of those that a mesh axis runs over, the one named last changes fastest.
Arguments:
- gate_inner: bfloat16 [256, 32768], P('ch', 'seq'), may hold values from -6 to 6
- values: bfloat16 [256, 32768], P('ch', 'seq'), may hold values from -6 to 6
- gate_outer: bfloat16 [256, 32768], P('ch', 'seq'), may hold values from -6 to 6
- filters: float32 [256, 32768], P('ch', 'seq'), may hold values from -1.2 to 1.2
- skip_bias: float32 [256], P('ch'), may hold values from 0.5 to 1.5
- out_weight: bfloat16 [256, 4096], replicated, may hold values from -0.375 to 0.375
Outputs:
- projected: bfloat16 [32768, 4096], P(('seq', 'ch'))
All inputs are finite; a program needn't handle non-finite values.
Results may differ from a plain program's by a relative error of at most 0.02.
Values may be sent and summed in bfloat16 or wider, within the bound.
A program may use at most 128 MiB of HBM per device.

v0:
```python
import functools

import jax
import jax.numpy as jnp
import numpy as np
from jax import lax
from jax.experimental import pallas as pl
from jax.experimental.pallas import tpu as pltpu
from jax.sharding import PartitionSpec as P

MESH = pl.DeviceIdType.MESH
LANES = 128
BF = jnp.bfloat16
F32 = jnp.float32


def tables(height):
    length = height * LANES
    low = np.arange(height)
    lane = np.arange(LANES)
    first = 2.0 * np.pi / (4 * height) * ((4 * low[:, None] + 1) * low[None, :] % (4 * height))
    twist = 2.0 * np.pi / (4 * length) * ((4 * low[:, None] + 1) * lane[None, :] % (4 * length))
    second = 2.0 * np.pi / LANES * (lane[:, None] * lane[None, :] % LANES)
    cos2, sin2 = np.cos(second), np.sin(second)
    fa = np.concatenate([np.cos(first), -np.sin(first)], 0)
    fb = np.block([[cos2, -sin2], [sin2, cos2]])
    gb = np.block([[cos2, sin2], [-sin2, cos2]]) / LANES
    ga = np.concatenate([np.cos(first.T), -np.sin(first.T)], 1) / height
    return (
        jnp.asarray(fa, BF),
        jnp.asarray(fb, BF),
        jnp.asarray(gb, BF),
        jnp.asarray(ga, BF),
        jnp.asarray(np.cos(twist), F32),
        jnp.asarray(np.sin(twist), F32),
    )


def mm(a, b):
    return jnp.dot(a, b, preferred_element_type=F32)


def convolve(x, f, fa, fb, gb, ga, tc, ts):
    height = x.shape[0]
    spread = mm(fa, jnp.concatenate([x, f], axis=1))
    xr, fr = spread[:height, :LANES], spread[:height, LANES:]
    xi, fi = spread[height:, :LANES], spread[height:, LANES:]
    rows_x = jnp.concatenate([xr * tc + xi * ts, xi * tc - xr * ts], axis=1)
    rows_f = jnp.concatenate([fr * tc + fi * ts, fi * tc - fr * ts], axis=1)
    sx = mm(rows_x.astype(BF), fb)
    sf = mm(rows_f.astype(BF), fb)
    xr, xi, fr, fi = sx[:, :LANES], sx[:, LANES:], sf[:, :LANES], sf[:, LANES:]
    prod = jnp.concatenate([xr * fr - xi * fi, xr * fi + xi * fr], axis=1).astype(BF)
    back = mm(prod, gb)
    br, bi = back[:, :LANES], back[:, LANES:]
    turned = jnp.concatenate([br * tc - bi * ts, bi * tc + br * ts], axis=0).astype(BF)
    return mm(ga, turned)


def kernel(
    n, nz, parts,
    gi, va, go, fl, skip, fa, fb, gb, ga, tc, ts,
    res,
    s_x, s_f, s_g, pack, got, conv, cin, gated, rz, tall,
    in_send, in_recv, out_send, out_recv, z_send, z_recv,
):
    me = lax.axis_index("seq")
    mz = lax.axis_index("ch")
    chans, toks = gi.shape
    tiles = toks // LANES
    own = chans // n
    cq = own // parts
    quarter = tiles // nz

    barrier = pltpu.get_barrier_semaphore()
    for k in range(1, n):
        pl.semaphore_signal(barrier, inc=1, device_id=(lax.rem(me + k, n), mz), device_id_type=MESH)
    for k in range(1, nz):
        pl.semaphore_signal(barrier, inc=1, device_id=(me, lax.rem(mz + k, nz)), device_id_type=MESH)

    @pl.loop(0, tiles)
    def _(t):
        cols = pl.ds(pl.multiple_of(t * LANES, LANES), LANES)
        rows = pl.ds(pl.multiple_of(t * chans, chans), chans)
        s_x[rows, :] = gi[:, cols].astype(F32) * va[:, cols].astype(F32)
        s_f[rows, :] = fl[:, cols]

    in_copies = []
    for q in range(parts):
        @pl.loop(0, n)
        def _(d):
            for i in range(cq):
                c = d * own + q * cq + i
                pack[q, d, i] = s_x[pl.ds(c, tiles, stride=chans), :].astype(BF)
                pack[q, d, cq + i] = s_f[pl.ds(c, tiles, stride=chans), :].astype(BF)

        if q == 0:
            pl.semaphore_wait(barrier, n - 1 + nz - 1)
        copies = []
        for k in range(1, n):
            d = lax.rem(me + k, n)
            copy = pltpu.make_async_remote_copy(
                src_ref=pack.at[q, d], dst_ref=got.at[q, me],
                send_sem=in_send.at[q, k], recv_sem=in_recv.at[q, k],
                device_id=(d, mz), device_id_type=MESH,
            )
            copy.start()
            copies.append(copy)
        in_copies.append(copies)
        got[q, me] = pack[q, me]

    @pl.loop(0, tiles)
    def _(t):
        cols = pl.ds(pl.multiple_of(t * LANES, LANES), LANES)
        rows = pl.ds(pl.multiple_of(t * chans, chans), chans)
        s_g[rows, :] = go[:, cols].astype(F32)

    out_copies = []
    for q in range(parts):
        for copy in in_copies[q]:
            copy.wait_recv()

        @pl.loop(0, cq)
        def _(i):
            x = got[q, :, i].reshape(n * tiles, LANES)
            f = got[q, :, cq + i].reshape(n * tiles, LANES)
            y = convolve(x, f, fa[...], fb[...], gb[...], ga[...], tc[...], ts[...])
            conv[q, :, i] = y.astype(BF).reshape(n, tiles, LANES)

        copies = []
        for k in range(1, n):
            d = lax.rem(me + k, n)
            copy = pltpu.make_async_remote_copy(
                src_ref=conv.at[q, d], dst_ref=cin.at[q, me],
                send_sem=out_send.at[q, k], recv_sem=out_recv.at[q, k],
                device_id=(d, mz), device_id_type=MESH,
            )
            copy.start()
            copies.append(copy)
        out_copies.append(copies)
        cin[q, me] = conv[q, me]

    z_copies = []
    for q in range(parts):
        for copy in out_copies[q]:
            copy.wait_recv()

        @pl.loop(0, n)
        def _(d):
            for pair in range(cq // 2):
                both = []
                for i in (2 * pair, 2 * pair + 1):
                    c = d * own + q * cq + i
                    mixed = s_x[pl.ds(c, tiles, stride=chans), :]
                    outer = s_g[pl.ds(c, tiles, stride=chans), :]
                    both.append(outer * (cin[q, d, i].astype(F32) + skip[c] * mixed))
                for z in range(nz):
                    rows = slice(z * quarter, (z + 1) * quarter)
                    gated[q, z, d * (cq // 2) + pair] = jnp.concatenate(
                        [both[0][rows], both[1][rows]], axis=0
                    ).astype(BF)

        copies = []
        for k in range(1, nz):
            z = lax.rem(mz + k, nz)
            copy = pltpu.make_async_remote_copy(
                src_ref=gated.at[q, z], dst_ref=rz.at[q, mz],
                send_sem=z_send.at[q, k], recv_sem=z_recv.at[q, k],
                device_id=(me, z), device_id_type=MESH,
            )
            copy.start()
            copies.append(copy)
        z_copies.append(copies)
        rz[q, mz] = gated[q, mz]

    for q in range(parts):
        for copy in z_copies[q]:
            copy.wait_recv()

        @pl.loop(0, nz * n)
        def _(g):
            z, d = g // n, g % n
            block = rz[q, z, pl.ds(d * (cq // 2), cq // 2)].astype(F32)
            start = pl.multiple_of((g * own + q * cq) * quarter, cq * quarter)
            tall[pl.ds(start, cq * quarter), :] = block.reshape(cq * quarter, LANES)

    for j in range(quarter):
        res[:, j * LANES:(j + 1) * LANES] = tall[pl.ds(j, nz * chans, stride=quarter), :].astype(BF)

    for copies in in_copies + out_copies + z_copies:
        for copy in copies:
            copy.wait_send()


def regroup(n, nz, gate_inner, values, gate_outer, filters, skip_bias):
    chans, toks = gate_inner.shape
    tiles = toks // LANES
    own = chans // n
    parts = max(1, min(2, own // 2))
    cq = own // parts
    quarter = tiles // nz
    height = n * tiles
    vmem = pl.BlockSpec(memory_space=pltpu.VMEM)
    smem = pl.BlockSpec(memory_space=pltpu.SMEM)
    dma = pltpu.SemaphoreType.DMA
    return pl.pallas_call(
        functools.partial(kernel, n, nz, parts),
        out_shape=jax.ShapeDtypeStruct((nz * chans, toks // nz), BF),
        in_specs=[vmem] * 4 + [smem] + [vmem] * 6,
        out_specs=vmem,
        scratch_shapes=[
            pltpu.VMEM((tiles * chans, LANES), F32),
            pltpu.VMEM((tiles * chans, LANES), F32),
            pltpu.VMEM((tiles * chans, LANES), F32),
            pltpu.VMEM((parts, n, 2 * cq, tiles, LANES), BF),
            pltpu.VMEM((parts, n, 2 * cq, tiles, LANES), BF),
            pltpu.VMEM((parts, n, cq, tiles, LANES), BF),
            pltpu.VMEM((parts, n, cq, tiles, LANES), BF),
            pltpu.VMEM((parts, nz, n * cq // 2, 2 * quarter, LANES), BF),
            pltpu.VMEM((parts, nz, n * cq // 2, 2 * quarter, LANES), BF),
            pltpu.VMEM((nz * chans * quarter, LANES), F32),
            dma((parts, n)), dma((parts, n)),
            dma((parts, n)), dma((parts, n)),
            dma((parts, nz)), dma((parts, nz)),
        ],
        compiler_params=pltpu.CompilerParams(
            collective_id=0, has_side_effects=True, vmem_limit_bytes=50 * 2**20
        ),
        name="convolve_and_regroup",
    )(gate_inner, values, gate_outer, filters, skip_bias, *tables(height))


def shards(n, nz, gate_inner, values, gate_outer, filters, skip_bias, out_weight):
    regrouped = regroup(n, nz, gate_inner, values, gate_outer, filters, skip_bias)
    projected = lax.dot_general(
        regrouped, out_weight, (((0,), (0,)), ((), ())), preferred_element_type=F32
    )
    return projected.astype(BF)


def solution(mesh):
    n, nz = mesh.shape["seq"], mesh.shape["ch"]
    in_specs = (P("ch", "seq"), P("ch", "seq"), P("ch", "seq"), P("ch", "seq"), P("ch"), P())
    out_specs = P(("seq", "ch"), None)
    return jax.shard_map(
        functools.partial(shards, n, nz),
        mesh=mesh, in_specs=in_specs, out_specs=out_specs, check_vma=False,
    )
```

profile of v0, /device:TPU:0, one launch (start us, length us, event | category | flops | bytes accessed | tf_op | source)
XLA Modules:
  0.0 51.7 jit_solution(16685133073316570863)
XLA Ops:
  0.0 0.0 copy-start
  0.0 0.0 copy-start.1
  0.0 1.2 %copy-done.1 = bf16[64,4096]{1,0:T(8,128)(2,1)S(1)} copy-done((bf16[64,4096]{1,0:T(8,128)(2,1)S(1)}, bf16[64,4096]{1,0:T(8,128)(2,1)}, u32[]{:S(2)}) %copy-start.1) | copy-done | bytes 524312
  1.2 0.0 copy-start.2
  1.2 1.0 %copy-done.2 = bf16[64,4096]{1,0:T(8,128)(2,1)S(1)} copy-done((bf16[64,4096]{1,0:T(8,128)(2,1)S(1)}, bf16[64,4096]{1,0:T(8,128)(2,1)}, u32[]{:S(2)}) %copy-start.2) | copy-done | bytes 524312
  2.2 0.0 copy-start.3
  2.2 1.0 %copy-done.3 = bf16[64,4096]{1,0:T(8,128)(2,1)S(1)} copy-done((bf16[64,4096]{1,0:T(8,128)(2,1)S(1)}, bf16[64,4096]{1,0:T(8,128)(2,1)}, u32[]{:S(2)}) %copy-start.3) | copy-done | bytes 524312
  3.3 0.0 copy-start.4
  3.3 0.9 %copy-done.4 = bf16[256,512]{1,0:T(8,128)(2,1)S(1)} copy-done((bf16[256,512]{1,0:T(8,128)(2,1)S(1)}, bf16[256,512]{1,0:T(8,128)(2,1)}, u32[]{:S(2)}) %copy-start.4) | copy-done | bytes 262168
  4.2 0.0 copy-start.5
  4.2 0.9 %copy-done.5 = bf16[512,256]{1,0:T(8,128)(2,1)S(1)} copy-done((bf16[512,256]{1,0:T(8,128)(2,1)S(1)}, bf16[512,256]{1,0:T(8,128)(2,1)}, u32[]{:S(2)}) %copy-start.5) | copy-done | bytes 262168
  5.2 0.0 copy-start.6
  5.2 0.9 %copy-done.6 = f32[256,128]{1,0:T(8,128)S(1)} copy-done((f32[256,128]{1,0:T(8,128)S(1)}, f32[256,128]{1,0:T(8,128)}, u32[]{:S(2)}) %copy-start.6) | copy-done | bytes 131096
  6.1 0.0 copy-start.7
  6.1 0.9 %copy-done.7 = f32[256,128]{1,0:T(8,128)S(1)} copy-done((f32[256,128]{1,0:T(8,128)S(1)}, f32[256,128]{1,0:T(8,128)}, u32[]{:S(2)}) %copy-start.7) | copy-done | bytes 131096
  7.0 0.0 copy-start.8
  7.0 0.9 %copy-done.8 = bf16[256,256]{1,0:T(8,128)(2,1)S(1)} copy-done((bf16[256,256]{1,0:T(8,128)(2,1)S(1)}, bf16[256,256]{1,0:T(8,128)(2,1)}, u32[]{:S(2)}) %copy-start.8) | copy-done | bytes 131096
  7.9 0.0 copy-start.9
  7.9 0.9 %copy-done.9 = bf16[256,256]{1,0:T(8,128)(2,1)S(1)} copy-done((bf16[256,256]{1,0:T(8,128)(2,1)S(1)}, bf16[256,256]{1,0:T(8,128)(2,1)}, u32[]{:S(2)}) %copy-start.9) | copy-done | bytes 131096
  8.8 0.0 copy-start.10
  8.8 0.7 %copy-done.10 = f32[64]{0:T(128)S(1)} copy-done((f32[64]{0:T(128)S(1)}, f32[64]{0:T(128)}, u32[]{:S(2)}) %copy-start.10) | copy-done | bytes 280
  9.5 36.4 %convolve_and_regroup.1 = bf16[256,1024]{1,0:T(8,128)(2,1)S(1)} custom-call(bf16[64,4096]{1,0:T(8,128)(2,1)S(1)} %copy-done.1, bf16[64,4096]{1,0:T(8,128)(2,1)S(1)} %copy-done.2, bf16[64,4096]{1,0:T(8,128)(2,1)S(1)} %copy-done.3, f32[64,4096]{1,0:T(8,128)} %fl.1, f32[64]{0:T(128)S(1)} %copy-done.10, bf16[512,256]{1,0:T(8,128)(2,1)S(1)} %copy-done.5, ...), custom_call_target="tpu_custom_call" | custom-call | tf_op jit(solution)/shard_map/convolve_and_regroup/pallas_call | solution.py:206
  45.9 0.0 copy-done
  45.9 5.8 %convolution_convert_fusion = bf16[1024,4096]{1,0:T(8,128)(2,1)} fusion(bf16[256,1024]{1,0:T(8,128)(2,1)S(1)} %convolve_and_regroup.1, bf16[256,4096]{1,0:T(8,128)(2,1)S(1)} %copy-done), kind=kOutput, calls=%fused_computation | convolution fusion | flops 2151677952 | bytes 11010048 | tf_op jit(solution)/shard_map/dot_general | solution.py:235
Async XLA Ops:
  0.0 45.9 %copy-start = (bf16[256,4096]{1,0:T(8,128)(2,1)S(1)}, bf16[256,4096]{1,0:T(8,128)(2,1)}, u32[]{:S(2)}) copy-start(bf16[256,4096]{1,0:T(8,128)(2,1)} %param.17) | copy-start | bytes 6291460
  0.0 1.2 %copy-start.1 = (bf16[64,4096]{1,0:T(8,128)(2,1)S(1)}, bf16[64,4096]{1,0:T(8,128)(2,1)}, u32[]{:S(2)}) copy-start(bf16[64,4096]{1,0:T(8,128)(2,1)} %gi.1) | copy-start | bytes 1572868
  1.2 1.0 %copy-start.2 = (bf16[64,4096]{1,0:T(8,128)(2,1)S(1)}, bf16[64,4096]{1,0:T(8,128)(2,1)}, u32[]{:S(2)}) copy-start(bf16[64,4096]{1,0:T(8,128)(2,1)} %va.1) | copy-start | bytes 1572868
  2.2 1.0 %copy-start.3 = (bf16[64,4096]{1,0:T(8,128)(2,1)S(1)}, bf16[64,4096]{1,0:T(8,128)(2,1)}, u32[]{:S(2)}) copy-start(bf16[64,4096]{1,0:T(8,128)(2,1)} %go.1) | copy-start | bytes 1572868
  3.3 0.9 %copy-start.4 = (bf16[256,512]{1,0:T(8,128)(2,1)S(1)}, bf16[256,512]{1,0:T(8,128)(2,1)}, u32[]{:S(2)}) copy-start(bf16[256,512]{1,0:T(8,128)(2,1)} %constant.15.clone.ga) | copy-start | bytes 786436
  4.2 0.9 %copy-start.5 = (bf16[512,256]{1,0:T(8,128)(2,1)S(1)}, bf16[512,256]{1,0:T(8,128)(2,1)}, u32[]{:S(2)}) copy-start(bf16[512,256]{1,0:T(8,128)(2,1)} %constant.12.clone.fa) | copy-start | bytes 786436
  5.2 0.9 %copy-start.6 = (f32[256,128]{1,0:T(8,128)S(1)}, f32[256,128]{1,0:T(8,128)}, u32[]{:S(2)}) copy-start(f32[256,128]{1,0:T(8,128)} %constant.17.clone.ts) | copy-start | bytes 393220
  6.1 0.9 %copy-start.7 = (f32[256,128]{1,0:T(8,128)S(1)}, f32[256,128]{1,0:T(8,128)}, u32[]{:S(2)}) copy-start(f32[256,128]{1,0:T(8,128)} %constant.16.clone.tc) | copy-start | bytes 393220
  7.0 0.9 %copy-start.8 = (bf16[256,256]{1,0:T(8,128)(2,1)S(1)}, bf16[256,256]{1,0:T(8,128)(2,1)}, u32[]{:S(2)}) copy-start(bf16[256,256]{1,0:T(8,128)(2,1)} %constant.14.clone.gb) | copy-start | bytes 393220
  7.9 0.9 %copy-start.9 = (bf16[256,256]{1,0:T(8,128)(2,1)S(1)}, bf16[256,256]{1,0:T(8,128)(2,1)}, u32[]{:S(2)}) copy-start(bf16[256,256]{1,0:T(8,128)(2,1)} %constant.13.clone.fb) | copy-start | bytes 393220
  8.8 0.7 %copy-start.10 = (f32[64]{0:T(128)S(1)}, f32[64]{0:T(128)}, u32[]{:S(2)}) copy-start(f32[64]{0:T(128)} %skip.1) | copy-start | bytes 772
where the time goes:
time: 52 us; the launch traced here: 51.7 us
  Pallas kernels  36.4 us (70%)
  local copies, waits for them, and re-layouts  9.45 us (18%)
  matrix products  5.8 us (11%)
    pallas_call x1, Pallas kernels, regroup(): pl.pallas_call(functools.partial(kernel, n, nz, parts), out_shape=jax.Sha...  36.4 us
    unnamed x22, local copies, waits for them, and re-layouts  9.45 us
    dot_general x1, matrix products, shards(): lax.dot_general(regrouped, out_weight, (((0,), (0,)), ((), ())), preferre...  5.8 us

commit v1 on v0

v1 whole, which is shorter than its diff:
```python
import functools

import jax
import jax.numpy as jnp
import numpy as np
from jax import lax
from jax.experimental import pallas as pl
from jax.experimental.pallas import tpu as pltpu
from jax.sharding import PartitionSpec as P

MESH = pl.DeviceIdType.MESH
LANES = 128
BF = jnp.bfloat16
F32 = jnp.float32


def tables(height):
    length = height * LANES
    low = np.arange(height)
    lane = np.arange(LANES)
    first = 2.0 * np.pi / (4 * height) * ((4 * low[:, None] + 1) * low[None, :] % (4 * height))
    twist = 2.0 * np.pi / (4 * length) * ((4 * low[:, None] + 1) * lane[None, :] % (4 * length))
    second = 2.0 * np.pi / LANES * (lane[:, None] * lane[None, :] % LANES)
    cos2, sin2 = np.cos(second), np.sin(second)
    fa = np.concatenate([np.cos(first), -np.sin(first)], 0)
    fb = np.block([[cos2, -sin2], [sin2, cos2]])
    gb = np.block([[cos2, sin2], [-sin2, cos2]]) / LANES
    ga = np.concatenate([np.cos(first.T), -np.sin(first.T)], 1) / height
    return (
        jnp.asarray(fa, F32),
        jnp.asarray(fb, F32),
        jnp.asarray(gb, F32),
        jnp.asarray(ga, F32),
        jnp.asarray(np.cos(twist), F32),
        jnp.asarray(np.sin(twist), F32),
    )


def mm(a, b):
    return jnp.dot(a, b, preferred_element_type=F32)


def convolve(x, f, fa, fb, gb, ga, tc, ts):
    height = x.shape[0]
    spread = mm(fa, jnp.concatenate([x, f], axis=1))
    xr, fr = spread[:height, :LANES], spread[:height, LANES:]
    xi, fi = spread[height:, :LANES], spread[height:, LANES:]
    rows_x = jnp.concatenate([xr * tc + xi * ts, xi * tc - xr * ts], axis=1)
    rows_f = jnp.concatenate([fr * tc + fi * ts, fi * tc - fr * ts], axis=1)
    sx = mm(rows_x.astype(BF), fb)
    sf = mm(rows_f.astype(BF), fb)
    xr, xi, fr, fi = sx[:, :LANES], sx[:, LANES:], sf[:, :LANES], sf[:, LANES:]
    prod = jnp.concatenate([xr * fr - xi * fi, xr * fi + xi * fr], axis=1).astype(BF)
    back = mm(prod, gb)
    br, bi = back[:, :LANES], back[:, LANES:]
    turned = jnp.concatenate([br * tc - bi * ts, bi * tc + br * ts], axis=0).astype(BF)
    return mm(ga, turned)


def kernel(
    n, nz, parts, *refs,
):
    hbm, (out, weight), rest = refs[:12], refs[12:14], refs[14:]
    gi, va, fl, go, skip, wide_fa, wide_fb, wide_gb, wide_ga, tc, ts = rest[:11]
    fa, fb, gb, ga, s_x, s_f, s_g, pack, got, conv, cin, gated = rest[11:23]
    load, in_send, in_recv, out_send, out_recv, z_send, z_recv = rest[23:]
    me = lax.axis_index("seq")
    mz = lax.axis_index("ch")
    chans, toks = gi.shape
    tiles = toks // LANES
    own = chans // n
    cq = own // parts
    quarter = tiles // nz

    barrier = pltpu.get_barrier_semaphore()
    for k in range(1, n):
        pl.semaphore_signal(barrier, inc=1, device_id=(lax.rem(me + k, n), mz), device_id_type=MESH)
    for k in range(1, nz):
        pl.semaphore_signal(barrier, inc=1, device_id=(me, lax.rem(mz + k, nz)), device_id_type=MESH)
    loads = [pltpu.make_async_copy(hbm[i], rest[i], load.at[i]) for i in range(11)]
    loads.append(pltpu.make_async_copy(hbm[11], weight, load.at[11]))
    for copy in loads:
        copy.start()

    def fill(dst, value):
        @pl.loop(0, tiles, unroll=4)
        def _(t):
            cols = pl.ds(pl.multiple_of(t * LANES, LANES), LANES)
            rows = pl.ds(pl.multiple_of(t * chans, chans), chans)
            dst[rows, :] = value(cols)

    def start(src, dst, send, recv, device):
        copy = pltpu.make_async_remote_copy(
            src_ref=src, dst_ref=dst, send_sem=send, recv_sem=recv,
            device_id=device, device_id_type=MESH,
        )
        copy.start()
        return copy

    def send_in(q):
        @pl.loop(0, n, unroll=2)
        def _(d):
            for i in range(cq):
                c = d * own + q * cq + i
                pack[q, d, i] = s_x[pl.ds(c, tiles, stride=chans), :].astype(BF)
                pack[q, d, cq + i] = s_f[pl.ds(c, tiles, stride=chans), :].astype(BF)

        if q == 0:
            pl.semaphore_wait(barrier, n - 1 + nz - 1)
        copies = []
        for k in range(1, n):
            d = lax.rem(me + k, n)
            copies.append(
                start(pack.at[q, d], got.at[q, me], in_send.at[q, k], in_recv.at[q, k], (d, mz))
            )
        got[q, me] = pack[q, me]
        return copies

    def send_out(q):
        for copy in in_copies[q]:
            copy.wait_recv()
        for i in range(cq):
            x = got[q, :, i].reshape(n * tiles, LANES)
            f = got[q, :, cq + i].reshape(n * tiles, LANES)
            y = convolve(x, f, fa[...], fb[...], gb[...], ga[...], tc[...], ts[...])
            conv[q, :, i] = y.astype(BF).reshape(n, tiles, LANES)
        copies = []
        for k in range(1, n):
            d = lax.rem(me + k, n)
            copies.append(
                start(conv.at[q, d], cin.at[q, me], out_send.at[q, k], out_recv.at[q, k], (d, mz))
            )
        cin[q, me] = conv[q, me]
        return copies

    def send_z(q):
        for copy in out_copies[q]:
            copy.wait_recv()

        @pl.loop(0, n, unroll=2)
        def _(d):
            for pair in range(cq // 2):
                both = []
                for i in (2 * pair, 2 * pair + 1):
                    c = d * own + q * cq + i
                    mixed = s_x[pl.ds(c, tiles, stride=chans), :]
                    outer = s_g[pl.ds(c, tiles, stride=chans), :]
                    both.append(outer * (cin[q, d, i].astype(F32) + skip[c] * mixed))
                for z in range(nz):
                    rows = slice(z * quarter, (z + 1) * quarter)
                    gated[q, z, d * (cq // 2) + pair] = jnp.concatenate(
                        [both[0][rows], both[1][rows]], axis=0
                    ).astype(BF)

        copies = []
        for k in range(1, nz):
            z = lax.rem(mz + k, nz)
            copies.append(
                start(gated.at[q, z], out.at[q, mz], z_send.at[q, k], z_recv.at[q, k], (me, z))
            )
        out[q, mz] = gated[q, mz]
        return copies

    for i in range(2):
        loads[i].wait()
    fill(s_x, lambda cols: gi[:, cols].astype(F32) * va[:, cols].astype(F32))
    loads[2].wait()
    fill(s_f, lambda cols: fl[:, cols])
    in_copies, out_copies, z_copies = [], [], []
    for q in range(min(2, parts)):
        in_copies.append(send_in(q))
    for i in range(3, 11):
        loads[i].wait()
    fill(s_g, lambda cols: go[:, cols].astype(F32))
    for narrow, wide in ((fa, wide_fa), (fb, wide_fb), (gb, wide_gb), (ga, wide_ga)):
        narrow[...] = wide[...].astype(BF)
    for q in range(parts):
        out_copies.append(send_out(q))
        if q + 2 < parts:
            in_copies.append(send_in(q + 2))
        if q >= 1:
            z_copies.append(send_z(q - 1))
    z_copies.append(send_z(parts - 1))
    for copies in z_copies:
        for copy in copies:
            copy.wait_recv()
    for copies in in_copies + out_copies + z_copies:
        for copy in copies:
            copy.wait_send()
    loads[11].wait()


def regroup(n, nz, parts, gate_inner, values, gate_outer, filters, skip_bias, out_weight):
    chans, toks = gate_inner.shape
    tiles = toks // LANES
    cq = chans // n // parts
    quarter = tiles // nz
    operands = (gate_inner, values, filters, gate_outer, skip_bias, *tables(n * tiles))
    fixed = [pltpu.VMEM(a.shape, BF) for a in operands[5:9]]
    dma = pltpu.SemaphoreType.DMA
    local = [pltpu.VMEM(a.shape, a.dtype) for a in operands]
    local[4] = pltpu.SMEM(skip_bias.shape, F32)
    operands += (out_weight,)
    vmem = pl.BlockSpec(memory_space=pltpu.VMEM)
    return pl.pallas_call(
        functools.partial(kernel, n, nz, parts),
        out_shape=(
            jax.ShapeDtypeStruct((parts, nz, n * cq // 2, 2 * quarter, LANES), BF),
            jax.ShapeDtypeStruct(out_weight.shape, BF),
        ),
        in_specs=[pl.BlockSpec(memory_space=pltpu.HBM)] * len(operands),
        out_specs=(vmem, vmem),
        scratch_shapes=local + fixed + [
            pltpu.VMEM((tiles * chans, LANES), F32),
            pltpu.VMEM((tiles * chans, LANES), F32),
            pltpu.VMEM((tiles * chans, LANES), F32),
            pltpu.VMEM((parts, n, 2 * cq, tiles, LANES), BF),
            pltpu.VMEM((parts, n, 2 * cq, tiles, LANES), BF),
            pltpu.VMEM((parts, n, cq, tiles, LANES), BF),
            pltpu.VMEM((parts, n, cq, tiles, LANES), BF),
            pltpu.VMEM((parts, nz, n * cq // 2, 2 * quarter, LANES), BF),
            dma((len(operands),)),
            dma((parts, n)), dma((parts, n)),
            dma((parts, n)), dma((parts, n)),
            dma((parts, nz)), dma((parts, nz)),
        ],
        compiler_params=pltpu.CompilerParams(
            collective_id=0, has_side_effects=True, vmem_limit_bytes=44 * 2**20
        ),
        name="convolve_and_regroup",
    )(*[pltpu.with_memory_space_constraint(a, pltpu.HBM) for a in operands])


def project_kernel(n, blocks, weight, out, tall):
    parts, nz, pairs, double, _ = blocks.shape
    quarter = double // 2
    cp = pairs // n
    size = cp * double
    j = pl.program_id(0)

    @pl.when(j == 0)
    def _():
        for q in range(parts):
            @pl.loop(0, nz * n, unroll=2)
            def _(g):
                block = blocks[q, g // n, pl.ds(g % n * cp, cp)].astype(F32)
                first = pl.multiple_of((g * parts + q) * size, size)
                tall[pl.ds(first, size), :] = block.reshape(size, LANES)

    lhs = tall[pl.ds(j, weight.shape[0], stride=quarter), :].astype(BF)
    out[...] = lax.dot_general(
        lhs, weight[...], (((0,), (0,)), ((), ())), preferred_element_type=F32
    ).astype(BF)


def project(n, blocks, out_weight):
    quarter = blocks.shape[3] // 2
    depth, width = out_weight.shape
    vmem = pl.BlockSpec(memory_space=pltpu.VMEM)
    return pl.pallas_call(
        functools.partial(project_kernel, n),
        out_shape=jax.ShapeDtypeStruct((quarter * LANES, width), BF),
        grid=(quarter,),
        in_specs=[vmem, vmem],
        out_specs=pl.BlockSpec((LANES, width), lambda j: (j, 0)),
        scratch_shapes=[pltpu.VMEM((depth * quarter, LANES), F32)],
        compiler_params=pltpu.CompilerParams(vmem_limit_bytes=24 * 2**20),
        name="project",
    )(blocks, out_weight)


def shards(n, nz, gate_inner, values, gate_outer, filters, skip_bias, out_weight):
    parts = max(1, min(4, gate_inner.shape[0] // n // 2))
    blocks, weight = regroup(
        n, nz, parts, gate_inner, values, gate_outer, filters, skip_bias, out_weight
    )
    return project(n, blocks, weight)


def solution(mesh):
    n, nz = mesh.shape["seq"], mesh.shape["ch"]
    in_specs = (P("ch", "seq"), P("ch", "seq"), P("ch", "seq"), P("ch", "seq"), P("ch"), P())
    out_specs = P(("seq", "ch"), None)
    return jax.shard_map(
        functools.partial(shards, n, nz),
        mesh=mesh, in_specs=in_specs, out_specs=out_specs, check_vma=False,
    )
```

time: 52 us -> 42 us (0.81)
  local copies, waits for them, and re-layouts: 9.45 us -> 0 us
  matrix products: 5.8 us -> 0 us
  Pallas kernels: 36.4 us -> 41.9 us
    unnamed x22 -> x0, local copies, waits for them, and re-layouts: 9.45 us -> none
    dot_general x1 -> x0, matrix products: 5.8 us -> none  [shards(): lax.dot_general(regrouped, out_weight, (((0,), (0,)), ((), ())), preferre...]
    pallas_call x1 -> x2, Pallas kernels: 36.4 us -> 41.9 us  [the longest x1 34.4 us: regroup(): pl.pallas_call(functools.partial(kernel, n, nz, parts), out_shape=(jax.Sh...]
where the time goes in v1:
time: 42 us; the launch traced here: 41.9 us
  Pallas kernels  41.9 us (100%)
    pallas_call x1, Pallas kernels, regroup(): pl.pallas_call(functools.partial(kernel, n, nz, parts), out_shape=(jax.Sh...  34.4 us
    pallas_call x1, Pallas kernels, project(): pl.pallas_call(functools.partial(project_kernel, n), out_shape=jax.ShapeD...  7.51 us

profile of v1, /device:TPU:0, one launch (start us, length us, event | category | flops | bytes accessed | tf_op | source)
XLA Modules:
  0.0 41.9 jit_solution(6073224523562287716)
XLA Ops:
  0.0 34.4 %convolve_and_regroup.1 = (bf16[4,4,8,16,128]{4,3,2,1,0:T(8,128)(2,1)S(1)}, bf16[256,4096]{1,0:T(8,128)(2,1)S(1)}) custom-call(bf16[64,4096]{1,0:T(8,128)(2,1)} %refs_0_.1, bf16[64,4096]{1,0:T(8,128)(2,1)} %refs_1_.1, f32[64,4096]{1,0:T(8,128)} %refs_2_.1, bf16[64,4096]{1,0:T(8,128)(2,1)} %refs_3_.1, f32[64]{0:T(128)} %refs_4_.1, ...), custom_call_target="tpu_custom_call" | custom-call | tf_op jit(solution)/shard_map/convolve_and_regroup/pallas_call | solution.py:205
  34.4 7.5 %project.1 = bf16[1024,4096]{1,0:T(8,128)(2,1)} custom-call(bf16[4,4,8,16,128]{4,3,2,1,0:T(8,128)(2,1)S(1)} %get-tuple-element.7.blocks, bf16[256,4096]{1,0:T(8,128)(2,1)S(1)} %get-tuple-element.8.weight), custom_call_target="tpu_custom_call" | custom-call | tf_op jit(solution)/shard_map/project/pallas_call | solution.py:260

commit v2 on v1

--- a/solution.py
+++ b/solution.py
@@ -62,8 +62,8 @@
 ):
     hbm, (out, weight), rest = refs[:12], refs[12:14], refs[14:]
     gi, va, fl, go, skip, wide_fa, wide_fb, wide_gb, wide_ga, tc, ts = rest[:11]
-    fa, fb, gb, ga, s_x, s_f, s_g, pack, got, conv, cin, gated = rest[11:23]
-    load, in_send, in_recv, out_send, out_recv, z_send, z_recv = rest[23:]
+    fa, fb, gb, ga, s_x, s_f, s_g, pack, got, conv, cin, gated, rz, tall = rest[11:25]
+    row_load, load, in_send, in_recv, out_send, out_recv, z_send, z_recv = rest[25:]
     me = lax.axis_index("seq")
     mz = lax.axis_index("ch")
     chans, toks = gi.shape
@@ -71,23 +71,40 @@
     own = chans // n
     cq = own // parts
     quarter = tiles // nz
+    group = n * cq
 
     barrier = pltpu.get_barrier_semaphore()
     for k in range(1, n):
         pl.semaphore_signal(barrier, inc=1, device_id=(lax.rem(me + k, n), mz), device_id_type=MESH)
     for k in range(1, nz):
         pl.semaphore_signal(barrier, inc=1, device_id=(me, lax.rem(mz + k, nz)), device_id_type=MESH)
-    loads = [pltpu.make_async_copy(hbm[i], rest[i], load.at[i]) for i in range(11)]
-    loads.append(pltpu.make_async_copy(hbm[11], weight, load.at[11]))
-    for copy in loads:
+    row_loads = []
+    for q in range(parts):
+        rows = pl.ds(q * group, group)
+        row_loads.append([
+            pltpu.make_async_copy(hbm[i].at[rows], rest[i].at[rows], row_load.at[q, i])
+            for i in range(4)
+        ])
+    loads = [pltpu.make_async_copy(hbm[i], rest[i], load.at[i - 4]) for i in range(4, 11)]
+    loads.append(pltpu.make_async_copy(hbm[11], weight, load.at[7]))
+    for copies in row_loads:
+        for copy in copies[:3]:
+            copy.start()
+    for copy in loads[:-1]:
         copy.start()
-
-    def fill(dst, value):
+    for copies in row_loads:
+        copies[3].start()
+    loads[-1].start()
+
+    def fill(q, dst, value):
         @pl.loop(0, tiles, unroll=4)
         def _(t):
             cols = pl.ds(pl.multiple_of(t * LANES, LANES), LANES)
-            rows = pl.ds(pl.multiple_of(t * chans, chans), chans)
-            dst[rows, :] = value(cols)
+            first = pl.multiple_of((q * tiles + t) * group, group)
+            dst[pl.ds(first, group), :] = value(pl.ds(q * group, group), cols)
+
+    def lane_rows(src, q, c):
+        return src[pl.ds(q * tiles * group + c, tiles, stride=group), :]
 
     def start(src, dst, send, recv, device):
         copy = pltpu.make_async_remote_copy(
@@ -98,12 +115,16 @@
         return copy
 
     def send_in(q):
+        for copy in row_loads[q][:3]:
+            copy.wait()
+        fill(q, s_x, lambda rows, cols: gi[rows, cols].astype(F32) * va[rows, cols].astype(F32))
+        fill(q, s_f, lambda rows, cols: fl[rows, cols])
+
         @pl.loop(0, n, unroll=2)
         def _(d):
             for i in range(cq):
-                c = d * own + q * cq + i
-                pack[q, d, i] = s_x[pl.ds(c, tiles, stride=chans), :].astype(BF)
-                pack[q, d, cq + i] = s_f[pl.ds(c, tiles, stride=chans), :].astype(BF)
+                pack[q, d, i] = lane_rows(s_x, q, d * cq + i).astype(BF)
+                pack[q, d, cq + i] = lane_rows(s_f, q, d * cq + i).astype(BF)
 
         if q == 0:
             pl.semaphore_wait(barrier, n - 1 + nz - 1)
@@ -134,6 +155,8 @@
         return copies
 
     def send_z(q):
+        row_loads[q][3].wait()
+        fill(q, s_g, lambda rows, cols: go[rows, cols].astype(F32))
         for copy in out_copies[q]:
             copy.wait_recv()
 
@@ -142,10 +165,9 @@
             for pair in range(cq // 2):
                 both = []
                 for i in (2 * pair, 2 * pair + 1):
-                    c = d * own + q * cq + i
-                    mixed = s_x[pl.ds(c, tiles, stride=chans), :]
-                    outer = s_g[pl.ds(c, tiles, stride=chans), :]
-                    both.append(outer * (cin[q, d, i].astype(F32) + skip[c] * mixed))
+                    c = d * cq + i
+                    through = skip[q * group + c] * lane_rows(s_x, q, c)
+                    both.append(lane_rows(s_g, q, c) * (cin[q, d, i].astype(F32) + through))
                 for z in range(nz):
                     rows = slice(z * quarter, (z + 1) * quarter)
                     gated[q, z, d * (cq // 2) + pair] = jnp.concatenate(
@@ -156,22 +178,28 @@
         for k in range(1, nz):
             z = lax.rem(mz + k, nz)
             copies.append(
-                start(gated.at[q, z], out.at[q, mz], z_send.at[q, k], z_recv.at[q, k], (me, z))
+                start(gated.at[q, z], rz.at[q, mz], z_send.at[q, k], z_recv.at[q, k], (me, z))
             )
-        out[q, mz] = gated[q, mz]
+        rz[q, mz] = gated[q, mz]
         return copies
 
-    for i in range(2):
-        loads[i].wait()
-    fill(s_x, lambda cols: gi[:, cols].astype(F32) * va[:, cols].astype(F32))
-    loads[2].wait()
-    fill(s_f, lambda cols: fl[:, cols])
+    def finish(q):
+        for copy in z_copies[q]:
+            copy.wait_recv()
+        tall[...] = rz[q].astype(F32).reshape(tall.shape)
+        for z in range(nz):
+            rows = slice(z * chans + q * group, z * chans + (q + 1) * group)
+            for j in range(quarter):
+                first = z * group * quarter + j
+                out[rows, j * LANES:(j + 1) * LANES] = tall[
+                    pl.ds(first, group, stride=quarter), :
+                ].astype(BF)
+
     in_copies, out_copies, z_copies = [], [], []
     for q in range(min(2, parts)):
         in_copies.append(send_in(q))
-    for i in range(3, 11):
-        loads[i].wait()
-    fill(s_g, lambda cols: go[:, cols].astype(F32))
+    for copy in loads[:-1]:
+        copy.wait()
     for narrow, wide in ((fa, wide_fa), (fb, wide_fb), (gb, wide_gb), (ga, wide_ga)):
         narrow[...] = wide[...].astype(BF)
     for q in range(parts):
@@ -181,13 +209,12 @@
         if q >= 1:
             z_copies.append(send_z(q - 1))
     z_copies.append(send_z(parts - 1))
-    for copies in z_copies:
-        for copy in copies:
-            copy.wait_recv()
+    for q in range(parts):
+        finish(q)
     for copies in in_copies + out_copies + z_copies:
         for copy in copies:
             copy.wait_send()
-    loads[11].wait()
+    loads[-1].wait()
 
 
 def regroup(n, nz, parts, gate_inner, values, gate_outer, filters, skip_bias, out_weight):
@@ -205,7 +232,7 @@
     return pl.pallas_call(
         functools.partial(kernel, n, nz, parts),
         out_shape=(
-            jax.ShapeDtypeStruct((parts, nz, n * cq // 2, 2 * quarter, LANES), BF),
+            jax.ShapeDtypeStruct((nz * chans, toks // nz), BF),
             jax.ShapeDtypeStruct(out_weight.shape, BF),
         ),
         in_specs=[pl.BlockSpec(memory_space=pltpu.HBM)] * len(operands),
@@ -219,7 +246,10 @@
             pltpu.VMEM((parts, n, cq, tiles, LANES), BF),
             pltpu.VMEM((parts, n, cq, tiles, LANES), BF),
             pltpu.VMEM((parts, nz, n * cq // 2, 2 * quarter, LANES), BF),
-            dma((len(operands),)),
+            pltpu.VMEM((parts, nz, n * cq // 2, 2 * quarter, LANES), BF),
+            pltpu.VMEM((nz * n * cq * quarter, LANES), F32),
+            dma((parts, 4)),
+            dma((8,)),
             dma((parts, n)), dma((parts, n)),
             dma((parts, n)), dma((parts, n)),
             dma((parts, nz)), dma((parts, nz)),
@@ -231,50 +261,43 @@
     )(*[pltpu.with_memory_space_constraint(a, pltpu.HBM) for a in operands])
 
 
-def project_kernel(n, blocks, weight, out, tall):
-    parts, nz, pairs, double, _ = blocks.shape
-    quarter = double // 2
-    cp = pairs // n
-    size = cp * double
+def project_kernel(lhs, weight, out, rows):
+    width = out.shape[1]
     j = pl.program_id(0)
 
     @pl.when(j == 0)
     def _():
-        for q in range(parts):
-            @pl.loop(0, nz * n, unroll=2)
-            def _(g):
-                block = blocks[q, g // n, pl.ds(g % n * cp, cp)].astype(F32)
-                first = pl.multiple_of((g * parts + q) * size, size)
-                tall[pl.ds(first, size), :] = block.reshape(size, LANES)
-
-    lhs = tall[pl.ds(j, weight.shape[0], stride=quarter), :].astype(BF)
-    out[...] = lax.dot_general(
-        lhs, weight[...], (((0,), (0,)), ((), ())), preferred_element_type=F32
-    ).astype(BF)
-
-
-def project(n, blocks, out_weight):
-    quarter = blocks.shape[3] // 2
-    depth, width = out_weight.shape
+        for k in range(rows.shape[0] // LANES):
+            part = slice(k * LANES, (k + 1) * LANES)
+            rows[part, :] = lhs[:, part].astype(F32).T.astype(BF)
+
+    cols = pl.ds(pl.multiple_of(j * width, width), width)
+    out[...] = mm(rows[...], weight[:, cols]).astype(BF)
+
+
+def project(lhs, weight):
+    depth, height = lhs.shape
+    width = weight.shape[1]
+    block = min(512, width)
     vmem = pl.BlockSpec(memory_space=pltpu.VMEM)
     return pl.pallas_call(
-        functools.partial(project_kernel, n),
-        out_shape=jax.ShapeDtypeStruct((quarter * LANES, width), BF),
-        grid=(quarter,),
+        project_kernel,
+        out_shape=jax.ShapeDtypeStruct((height, width), BF),
+        grid=(width // block,),
         in_specs=[vmem, vmem],
-        out_specs=pl.BlockSpec((LANES, width), lambda j: (j, 0)),
-        scratch_shapes=[pltpu.VMEM((depth * quarter, LANES), F32)],
+        out_specs=pl.BlockSpec((height, block), lambda j: (0, j)),
+        scratch_shapes=[pltpu.VMEM((height, depth), BF)],
         compiler_params=pltpu.CompilerParams(vmem_limit_bytes=24 * 2**20),
         name="project",
-    )(blocks, out_weight)
+    )(lhs, weight)
 
 
 def shards(n, nz, gate_inner, values, gate_outer, filters, skip_bias, out_weight):
     parts = max(1, min(4, gate_inner.shape[0] // n // 2))
-    blocks, weight = regroup(
+    lhs, weight = regroup(
         n, nz, parts, gate_inner, values, gate_outer, filters, skip_bias, out_weight
     )
-    return project(n, blocks, weight)
+    return project(lhs, weight)
 
 
 def solution(mesh):

time: 42 us -> 40.5 us (0.964)
  Pallas kernels: 41.9 us -> 40.3 us
    pallas_call x1, Pallas kernels: 7.51 us -> 6.31 us  [project(): pl.pallas_call(project_kernel, out_shape=jax.ShapeDtypeStruct((height, wi...]
where the time goes in v2:
time: 40.5 us; the launch traced here: 40.4 us
  Pallas kernels  40.3 us (100%)
    pallas_call x1, Pallas kernels, regroup(): pl.pallas_call(functools.partial(kernel, n, nz, parts), out_shape=(jax.Sh...  34 us
    pallas_call x1, Pallas kernels, project(): pl.pallas_call(project_kernel, out_shape=jax.ShapeDtypeStruct((height, wi...  6.31 us

profile of v2, /device:TPU:0, one launch (start us, length us, event | category | flops | bytes accessed | tf_op | source)
XLA Modules:
  0.0 40.4 jit_solution(3664271589395766435)
XLA Ops:
  0.0 34.0 %convolve_and_regroup.1 = (bf16[256,1024]{1,0:T(8,128)(2,1)S(1)}, bf16[256,4096]{1,0:T(8,128)(2,1)S(1)}) custom-call(bf16[64,4096]{1,0:T(8,128)(2,1)} %refs_0_.1, bf16[64,4096]{1,0:T(8,128)(2,1)} %refs_1_.1, f32[64,4096]{1,0:T(8,128)} %refs_2_.1, bf16[64,4096]{1,0:T(8,128)(2,1)} %refs_3_.1, f32[64]{0:T(128)} %refs_4_.1, f32[512,256]{1,0:T(8,128)} %constant.12.clone.refs_5_, ...), custom_call_target="tpu_custom_call" | custom-call | tf_op jit(solution)/shard_map/convolve_and_regroup/pallas_call | solution.py:232
  34.0 6.3 %project.1 = bf16[1024,4096]{1,0:T(8,128)(2,1)} custom-call(bf16[256,1024]{1,0:T(8,128)(2,1)S(1)} %get-tuple-element.7.lhs, bf16[256,4096]{1,0:T(8,128)(2,1)S(1)} %get-tuple-element.8.weight), custom_call_target="tpu_custom_call" | custom-call | tf_op jit(solution)/shard_map/project/pallas_call | solution.py:283

commit v3 on v2

--- a/solution.py
+++ b/solution.py
@@ -196,7 +196,7 @@
                 ].astype(BF)
 
     in_copies, out_copies, z_copies = [], [], []
-    for q in range(min(2, parts)):
+    for q in range(min(3, parts)):
         in_copies.append(send_in(q))
     for copy in loads[:-1]:
         copy.wait()
@@ -204,8 +204,8 @@
         narrow[...] = wide[...].astype(BF)
     for q in range(parts):
         out_copies.append(send_out(q))
-        if q + 2 < parts:
-            in_copies.append(send_in(q + 2))
+        if q + 3 < parts:
+            in_copies.append(send_in(q + 3))
         if q >= 1:
             z_copies.append(send_z(q - 1))
     z_copies.append(send_z(parts - 1))
@@ -278,7 +278,7 @@
 def project(lhs, weight):
     depth, height = lhs.shape
     width = weight.shape[1]
-    block = min(512, width)
+    block = min(256, width)
     vmem = pl.BlockSpec(memory_space=pltpu.VMEM)
     return pl.pallas_call(
         project_kernel,

time: 40.5 us -> 42.7 us (1.054)
  Pallas kernels: 40.3 us -> 42.5 us
    pallas_call x1, Pallas kernels: 6.31 us -> 9.34 us  [project(): pl.pallas_call(project_kernel, out_shape=jax.ShapeDtypeStruct((height, wi...]
    pallas_call x1, Pallas kernels: 34 us -> 33.2 us  [regroup(): pl.pallas_call(functools.partial(kernel, n, nz, parts), out_shape=(jax.Sh...]
where the time goes in v3:
time: 42.7 us; the launch traced here: 42.6 us
  Pallas kernels  42.5 us (100%)
    pallas_call x1, Pallas kernels, regroup(): pl.pallas_call(functools.partial(kernel, n, nz, parts), out_shape=(jax.Sh...  33.2 us
    pallas_call x1, Pallas kernels, project(): pl.pallas_call(project_kernel, out_shape=jax.ShapeDtypeStruct((height, wi...  9.34 us

profile of v3, /device:TPU:0, one launch (start us, length us, event | category | flops | bytes accessed | tf_op | source)
XLA Modules:
  0.0 42.6 jit_solution(14296018058757990696)
XLA Ops:
  0.0 33.2 %convolve_and_regroup.1 = (bf16[256,1024]{1,0:T(8,128)(2,1)S(1)}, bf16[256,4096]{1,0:T(8,128)(2,1)S(1)}) custom-call(bf16[64,4096]{1,0:T(8,128)(2,1)} %refs_0_.1, bf16[64,4096]{1,0:T(8,128)(2,1)} %refs_1_.1, f32[64,4096]{1,0:T(8,128)} %refs_2_.1, bf16[64,4096]{1,0:T(8,128)(2,1)} %refs_3_.1, f32[64]{0:T(128)} %refs_4_.1, f32[512,256]{1,0:T(8,128)} %constant.12.clone.refs_5_, ...), custom_call_target="tpu_custom_call" | custom-call | tf_op jit(solution)/shard_map/convolve_and_regroup/pallas_call | solution.py:232
  33.2 9.3 %project.1 = bf16[1024,4096]{1,0:T(8,128)(2,1)} custom-call(bf16[256,1024]{1,0:T(8,128)(2,1)S(1)} %get-tuple-element.7.lhs, bf16[256,4096]{1,0:T(8,128)(2,1)S(1)} %get-tuple-element.8.weight), custom_call_target="tpu_custom_call" | custom-call | tf_op jit(solution)/shard_map/project/pallas_call | solution.py:283

commit v4 on v2

--- a/solution.py
+++ b/solution.py
@@ -58,7 +58,7 @@
 
 
 def kernel(
-    n, nz, parts, *refs,
+    n, nz, parts, subs, *refs,
 ):
     hbm, (out, weight), rest = refs[:12], refs[12:14], refs[14:]
     gi, va, fl, go, skip, wide_fa, wide_fb, wide_gb, wide_ga, tc, ts = rest[:11]
@@ -68,10 +68,9 @@
     mz = lax.axis_index("ch")
     chans, toks = gi.shape
     tiles = toks // LANES
-    own = chans // n
-    cq = own // parts
     quarter = tiles // nz
-    group = n * cq
+    group = n * subs
+    chunks = parts * subs
 
     barrier = pltpu.get_barrier_semaphore()
     for k in range(1, n):
@@ -103,8 +102,9 @@
             first = pl.multiple_of((q * tiles + t) * group, group)
             dst[pl.ds(first, group), :] = value(pl.ds(q * group, group), cols)
 
-    def lane_rows(src, q, c):
-        return src[pl.ds(q * tiles * group + c, tiles, stride=group), :]
+    def lane_rows(src, q, d):
+        first = q // subs * tiles * group + q % subs * n
+        return src[pl.ds(first + d, tiles, stride=group), :]
 
     def start(src, dst, send, recv, device):
         copy = pltpu.make_async_remote_copy(
@@ -115,16 +115,17 @@
         return copy
 
     def send_in(q):
-        for copy in row_loads[q][:3]:
-            copy.wait()
-        fill(q, s_x, lambda rows, cols: gi[rows, cols].astype(F32) * va[rows, cols].astype(F32))
-        fill(q, s_f, lambda rows, cols: fl[rows, cols])
+        g = q // subs
+        if q % subs == 0:
+            for copy in row_loads[g][:3]:
+                copy.wait()
+            fill(g, s_x, lambda rows, cols: gi[rows, cols].astype(F32) * va[rows, cols].astype(F32))
+            fill(g, s_f, lambda rows, cols: fl[rows, cols])
 
         @pl.loop(0, n, unroll=2)
         def _(d):
-            for i in range(cq):
-                pack[q, d, i] = lane_rows(s_x, q, d * cq + i).astype(BF)
-                pack[q, d, cq + i] = lane_rows(s_f, q, d * cq + i).astype(BF)
+            pack[q, d, 0] = lane_rows(s_x, q, d).astype(BF)
+            pack[q, d, 1] = lane_rows(s_f, q, d).astype(BF)
 
         if q == 0:
             pl.semaphore_wait(barrier, n - 1 + nz - 1)
@@ -140,11 +141,10 @@
     def send_out(q):
         for copy in in_copies[q]:
             copy.wait_recv()
-        for i in range(cq):
-            x = got[q, :, i].reshape(n * tiles, LANES)
-            f = got[q, :, cq + i].reshape(n * tiles, LANES)
-            y = convolve(x, f, fa[...], fb[...], gb[...], ga[...], tc[...], ts[...])
-            conv[q, :, i] = y.astype(BF).reshape(n, tiles, LANES)
+        x = got[q, :, 0].reshape(n * tiles, LANES)
+        f = got[q, :, 1].reshape(n * tiles, LANES)
+        y = convolve(x, f, fa[...], fb[...], gb[...], ga[...], tc[...], ts[...])
+        conv[q] = y.astype(BF).reshape(n, tiles, LANES)
         copies = []
         for k in range(1, n):
             d = lax.rem(me + k, n)
@@ -155,24 +155,22 @@
         return copies
 
     def send_z(q):
-        row_loads[q][3].wait()
-        fill(q, s_g, lambda rows, cols: go[rows, cols].astype(F32))
+        g = q // subs
+        if q % subs == 0:
+            row_loads[g][3].wait()
+            fill(g, s_g, lambda rows, cols: go[rows, cols].astype(F32))
         for copy in out_copies[q]:
             copy.wait_recv()
 
-        @pl.loop(0, n, unroll=2)
-        def _(d):
-            for pair in range(cq // 2):
-                both = []
-                for i in (2 * pair, 2 * pair + 1):
-                    c = d * cq + i
-                    through = skip[q * group + c] * lane_rows(s_x, q, c)
-                    both.append(lane_rows(s_g, q, c) * (cin[q, d, i].astype(F32) + through))
-                for z in range(nz):
-                    rows = slice(z * quarter, (z + 1) * quarter)
-                    gated[q, z, d * (cq // 2) + pair] = jnp.concatenate(
-                        [both[0][rows], both[1][rows]], axis=0
-                    ).astype(BF)
+        @pl.loop(0, n // 2, unroll=2)
+        def _(pair):
+            both = []
+            for d in (2 * pair, 2 * pair + 1):
+                through = skip[q * n + d] * lane_rows(s_x, q, d)
+                both.append(lane_rows(s_g, q, d) * (cin[q, d].astype(F32) + through))
+            for z in range(nz):
+                rows = slice(z * quarter, (z + 1) * quarter)
+                gated[q, z, pair] = jnp.concatenate([both[0][rows], both[1][rows]], axis=0).astype(BF)
 
         copies = []
         for k in range(1, nz):
@@ -183,12 +181,16 @@
         rz[q, mz] = gated[q, mz]
         return copies
 
-    def finish(q):
-        for copy in z_copies[q]:
-            copy.wait_recv()
-        tall[...] = rz[q].astype(F32).reshape(tall.shape)
+    def finish(g):
+        for i in range(subs):
+            q = g * subs + i
+            for copy in z_copies[q]:
+                copy.wait_recv()
+            for z in range(nz):
+                rows = slice((z * subs + i) * n * quarter, (z * subs + i + 1) * n * quarter)
+                tall[rows, :] = rz[q, z].astype(F32).reshape(n * quarter, LANES)
         for z in range(nz):
-            rows = slice(z * chans + q * group, z * chans + (q + 1) * group)
+            rows = slice(z * chans + g * group, z * chans + (g + 1) * group)
             for j in range(quarter):
                 first = z * group * quarter + j
                 out[rows, j * LANES:(j + 1) * LANES] = tall[
@@ -196,31 +198,32 @@
                 ].astype(BF)
 
     in_copies, out_copies, z_copies = [], [], []
-    for q in range(min(2, parts)):
+    ahead = min(4, chunks)
+    for q in range(ahead):
         in_copies.append(send_in(q))
     for copy in loads[:-1]:
         copy.wait()
     for narrow, wide in ((fa, wide_fa), (fb, wide_fb), (gb, wide_gb), (ga, wide_ga)):
         narrow[...] = wide[...].astype(BF)
-    for q in range(parts):
+    for q in range(chunks):
         out_copies.append(send_out(q))
-        if q + 2 < parts:
-            in_copies.append(send_in(q + 2))
+        if q + ahead < chunks:
+            in_copies.append(send_in(q + ahead))
         if q >= 1:
             z_copies.append(send_z(q - 1))
-    z_copies.append(send_z(parts - 1))
-    for q in range(parts):
-        finish(q)
+    z_copies.append(send_z(chunks - 1))
+    for g in range(parts):
+        finish(g)
     for copies in in_copies + out_copies + z_copies:
         for copy in copies:
             copy.wait_send()
     loads[-1].wait()
 
 
-def regroup(n, nz, parts, gate_inner, values, gate_outer, filters, skip_bias, out_weight):
+def regroup(n, nz, parts, subs, gate_inner, values, gate_outer, filters, skip_bias, out_weight):
     chans, toks = gate_inner.shape
     tiles = toks // LANES
-    cq = chans // n // parts
+    chunks = parts * subs
     quarter = tiles // nz
     operands = (gate_inner, values, filters, gate_outer, skip_bias, *tables(n * tiles))
     fixed = [pltpu.VMEM(a.shape, BF) for a in operands[5:9]]
@@ -230,7 +233,7 @@
     operands += (out_weight,)
     vmem = pl.BlockSpec(memory_space=pltpu.VMEM)
     return pl.pallas_call(
-        functools.partial(kernel, n, nz, parts),
+        functools.partial(kernel, n, nz, parts, subs),
         out_shape=(
             jax.ShapeDtypeStruct((nz * chans, toks // nz), BF),
             jax.ShapeDtypeStruct(out_weight.shape, BF),
@@ -241,18 +244,18 @@
             pltpu.VMEM((tiles * chans, LANES), F32),
             pltpu.VMEM((tiles * chans, LANES), F32),
             pltpu.VMEM((tiles * chans, LANES), F32),
-            pltpu.VMEM((parts, n, 2 * cq, tiles, LANES), BF),
-            pltpu.VMEM((parts, n, 2 * cq, tiles, LANES), BF),
-            pltpu.VMEM((parts, n, cq, tiles, LANES), BF),
-            pltpu.VMEM((parts, n, cq, tiles, LANES), BF),
-            pltpu.VMEM((parts, nz, n * cq // 2, 2 * quarter, LANES), BF),
-            pltpu.VMEM((parts, nz, n * cq // 2, 2 * quarter, LANES), BF),
-            pltpu.VMEM((nz * n * cq * quarter, LANES), F32),
+            pltpu.VMEM((chunks, n, 2, tiles, LANES), BF),
+            pltpu.VMEM((chunks, n, 2, tiles, LANES), BF),
+            pltpu.VMEM((chunks, n, tiles, LANES), BF),
+            pltpu.VMEM((chunks, n, tiles, LANES), BF),
+            pltpu.VMEM((chunks, nz, n // 2, 2 * quarter, LANES), BF),
+            pltpu.VMEM((chunks, nz, n // 2, 2 * quarter, LANES), BF),
+            pltpu.VMEM((nz * n * subs * quarter, LANES), F32),
             dma((parts, 4)),
             dma((8,)),
-            dma((parts, n)), dma((parts, n)),
-            dma((parts, n)), dma((parts, n)),
-            dma((parts, nz)), dma((parts, nz)),
+            dma((chunks, n)), dma((chunks, n)),
+            dma((chunks, n)), dma((chunks, n)),
+            dma((chunks, nz)), dma((chunks, nz)),
         ],
         compiler_params=pltpu.CompilerParams(
             collective_id=0, has_side_effects=True, vmem_limit_bytes=44 * 2**20
@@ -261,18 +264,27 @@
     )(*[pltpu.with_memory_space_constraint(a, pltpu.HBM) for a in operands])
 
 
-def project_kernel(lhs, weight, out, rows):
-    width = out.shape[1]
-    j = pl.program_id(0)
-
-    @pl.when(j == 0)
-    def _():
-        for k in range(rows.shape[0] // LANES):
-            part = slice(k * LANES, (k + 1) * LANES)
-            rows[part, :] = lhs[:, part].astype(F32).T.astype(BF)
-
-    cols = pl.ds(pl.multiple_of(j * width, width), width)
-    out[...] = mm(rows[...], weight[:, cols]).astype(BF)
+def project_kernel(lhs, weight, out, rows, done, sem):
+    blocks, _, width = done.shape
+
+    @pl.loop(0, rows.shape[0] // LANES, unroll=2)
+    def _(k):
+        part = pl.ds(pl.multiple_of(k * LANES, LANES), LANES)
+        rows[part, :] = lhs[:, part].astype(F32).T.astype(BF)
+
+    def write(j):
+        cols = pl.ds(pl.multiple_of(j * width, width), width)
+        return pltpu.make_async_copy(done.at[j], out.at[:, cols], sem.at[j])
+
+    @pl.loop(0, blocks)
+    def _(j):
+        cols = pl.ds(pl.multiple_of(j * width, width), width)
+        done[j] = mm(rows[...], weight[:, cols]).astype(BF)
+        write(j).start()
+
+    @pl.loop(0, blocks)
+    def _(j):
+        write(j).wait()
 
 
 def project(lhs, weight):
@@ -283,19 +295,24 @@
     return pl.pallas_call(
         project_kernel,
         out_shape=jax.ShapeDtypeStruct((height, width), BF),
-        grid=(width // block,),
         in_specs=[vmem, vmem],
-        out_specs=pl.BlockSpec((height, block), lambda j: (0, j)),
-        scratch_shapes=[pltpu.VMEM((height, depth), BF)],
-        compiler_params=pltpu.CompilerParams(vmem_limit_bytes=24 * 2**20),
+        out_specs=pl.BlockSpec(memory_space=pltpu.HBM),
+        scratch_shapes=[
+            pltpu.VMEM((height, depth), BF),
+            pltpu.VMEM((width // block, height, block), BF),
+            pltpu.SemaphoreType.DMA((width // block,)),
+        ],
+        compiler_params=pltpu.CompilerParams(vmem_limit_bytes=32 * 2**20),
         name="project",
     )(lhs, weight)
 
 
 def shards(n, nz, gate_inner, values, gate_outer, filters, skip_bias, out_weight):
-    parts = max(1, min(4, gate_inner.shape[0] // n // 2))
+    own = gate_inner.shape[0] // n
+    parts = max(1, own // 2)
+    subs = own // parts
     lhs, weight = regroup(
-        n, nz, parts, gate_inner, values, gate_outer, filters, skip_bias, out_weight
+        n, nz, parts, subs, gate_inner, values, gate_outer, filters, skip_bias, out_weight
     )
     return project(lhs, weight)
 

time: 40.5 us -> 41.1 us (1.015)
  Pallas kernels: 40.3 us -> 41 us
    pallas_call x1, Pallas kernels: 34 us -> 36 us  [regroup(): pl.pallas_call(functools.partial(kernel, n, nz, parts, subs), out_shape=(...]
    pallas_call x1, Pallas kernels: 6.31 us -> 4.97 us  [project(): pl.pallas_call(project_kernel, out_shape=jax.ShapeDtypeStruct((height, wi...]
where the time goes in v4:
time: 41.1 us; the launch traced here: 41 us
  Pallas kernels  41 us (100%)
    pallas_call x1, Pallas kernels, regroup(): pl.pallas_call(functools.partial(kernel, n, nz, parts, subs), out_shape=(...  36 us
    pallas_call x1, Pallas kernels, project(): pl.pallas_call(project_kernel, out_shape=jax.ShapeDtypeStruct((height, wi...  4.97 us

profile of v4, /device:TPU:0, one launch (start us, length us, event | category | flops | bytes accessed | tf_op | source)
XLA Modules:
  0.0 41.0 jit_solution(14379797271230746225)
XLA Ops:
  0.0 36.0 %convolve_and_regroup.1 = (bf16[256,1024]{1,0:T(8,128)(2,1)S(1)}, bf16[256,4096]{1,0:T(8,128)(2,1)S(1)}) custom-call(bf16[64,4096]{1,0:T(8,128)(2,1)} %refs_0_.1, bf16[64,4096]{1,0:T(8,128)(2,1)} %refs_1_.1, f32[64,4096]{1,0:T(8,128)} %refs_2_.1, bf16[64,4096]{1,0:T(8,128)(2,1)} %refs_3_.1, f32[64]{0:T(128)} %refs_4_.1, f32[512,256]{1,0:T(8,128)} %constant.12.clone.refs_5_, ...), custom_call_target="tpu_custom_call" | custom-call | tf_op jit(solution)/shard_map/convolve_and_regroup/pallas_call | solution.py:235
  36.0 5.0 %project.1 = bf16[1024,4096]{1,0:T(8,128)(2,1)} custom-call(bf16[256,1024]{1,0:T(8,128)(2,1)S(1)} %get-tuple-element.7.lhs, bf16[256,4096]{1,0:T(8,128)(2,1)S(1)} %get-tuple-element.8.weight), custom_call_target="tpu_custom_call" | custom-call | tf_op jit(solution)/shard_map/project/pallas_call | solution.py:295

commit v5 on v3

--- a/solution.py
+++ b/solution.py
@@ -40,20 +40,31 @@
     return jnp.dot(a, b, preferred_element_type=F32)
 
 
-def convolve(x, f, fa, fb, gb, ga, tc, ts):
-    height = x.shape[0]
-    spread = mm(fa, jnp.concatenate([x, f], axis=1))
-    xr, fr = spread[:height, :LANES], spread[:height, LANES:]
-    xi, fi = spread[height:, :LANES], spread[height:, LANES:]
-    rows_x = jnp.concatenate([xr * tc + xi * ts, xi * tc - xr * ts], axis=1)
-    rows_f = jnp.concatenate([fr * tc + fi * ts, fi * tc - fr * ts], axis=1)
-    sx = mm(rows_x.astype(BF), fb)
-    sf = mm(rows_f.astype(BF), fb)
-    xr, xi, fr, fi = sx[:, :LANES], sx[:, LANES:], sf[:, :LANES], sf[:, LANES:]
+def convolve(signals, filters, fa, fb, gb, ga, tc, ts):
+    height = tc.shape[0]
+    count = len(signals)
+    spread = mm(fa, jnp.concatenate(signals + filters, axis=1))
+
+    def turn(k):
+        re = spread[:height, k * LANES:(k + 1) * LANES]
+        im = spread[height:, k * LANES:(k + 1) * LANES]
+        return jnp.concatenate([re * tc + im * ts, im * tc - re * ts], axis=1).astype(BF)
+
+    spectra = mm(jnp.concatenate([turn(k) for k in range(2 * count)], axis=0), fb)
+    half = count * height
+    xr, xi = spectra[:half, :LANES], spectra[:half, LANES:]
+    fr, fi = spectra[half:, :LANES], spectra[half:, LANES:]
     prod = jnp.concatenate([xr * fr - xi * fi, xr * fi + xi * fr], axis=1).astype(BF)
     back = mm(prod, gb)
-    br, bi = back[:, :LANES], back[:, LANES:]
-    turned = jnp.concatenate([br * tc - bi * ts, bi * tc + br * ts], axis=0).astype(BF)
+    real, imag = [], []
+    for k in range(count):
+        br = back[k * height:(k + 1) * height, :LANES]
+        bi = back[k * height:(k + 1) * height, LANES:]
+        real.append((br * tc - bi * ts).astype(BF))
+        imag.append((br * ts + bi * tc).astype(BF))
+    turned = jnp.concatenate(
+        [jnp.concatenate(real, axis=1), jnp.concatenate(imag, axis=1)], axis=0
+    )
     return mm(ga, turned)
 
 
@@ -140,11 +151,11 @@
     def send_out(q):
         for copy in in_copies[q]:
             copy.wait_recv()
+        flat = [got[q, :, i].reshape(n * tiles, LANES) for i in range(2 * cq)]
+        y = convolve(flat[:cq], flat[cq:], fa[...], fb[...], gb[...], ga[...], tc[...], ts[...])
         for i in range(cq):
-            x = got[q, :, i].reshape(n * tiles, LANES)
-            f = got[q, :, cq + i].reshape(n * tiles, LANES)
-            y = convolve(x, f, fa[...], fb[...], gb[...], ga[...], tc[...], ts[...])
-            conv[q, :, i] = y.astype(BF).reshape(n, tiles, LANES)
+            one = y[:, i * LANES:(i + 1) * LANES]
+            conv[q, :, i] = one.astype(BF).reshape(n, tiles, LANES)
         copies = []
         for k in range(1, n):
             d = lax.rem(me + k, n)
@@ -261,33 +272,45 @@
     )(*[pltpu.with_memory_space_constraint(a, pltpu.HBM) for a in operands])
 
 
-def project_kernel(lhs, weight, out, rows):
-    width = out.shape[1]
-    j = pl.program_id(0)
-
-    @pl.when(j == 0)
-    def _():
-        for k in range(rows.shape[0] // LANES):
-            part = slice(k * LANES, (k + 1) * LANES)
-            rows[part, :] = lhs[:, part].astype(F32).T.astype(BF)
-
-    cols = pl.ds(pl.multiple_of(j * width, width), width)
-    out[...] = mm(rows[...], weight[:, cols]).astype(BF)
+def project_kernel(lhs, weight, out, rows, done, sem):
+    blocks, _, width = done.shape
+
+    @pl.loop(0, rows.shape[0] // LANES, unroll=2)
+    def _(k):
+        part = pl.ds(pl.multiple_of(k * LANES, LANES), LANES)
+        rows[part, :] = lhs[:, part].astype(F32).T.astype(BF)
+
+    def write(j):
+        cols = pl.ds(pl.multiple_of(j * width, width), width)
+        return pltpu.make_async_copy(done.at[j], out.at[:, cols], sem.at[j])
+
+    @pl.loop(0, blocks)
+    def _(j):
+        cols = pl.ds(pl.multiple_of(j * width, width), width)
+        done[j] = mm(rows[...], weight[:, cols]).astype(BF)
+        write(j).start()
+
+    @pl.loop(0, blocks)
+    def _(j):
+        write(j).wait()
 
 
 def project(lhs, weight):
     depth, height = lhs.shape
     width = weight.shape[1]
-    block = min(256, width)
+    block = min(512, width)
     vmem = pl.BlockSpec(memory_space=pltpu.VMEM)
     return pl.pallas_call(
         project_kernel,
         out_shape=jax.ShapeDtypeStruct((height, width), BF),
-        grid=(width // block,),
         in_specs=[vmem, vmem],
-        out_specs=pl.BlockSpec((height, block), lambda j: (0, j)),
-        scratch_shapes=[pltpu.VMEM((height, depth), BF)],
-        compiler_params=pltpu.CompilerParams(vmem_limit_bytes=24 * 2**20),
+        out_specs=pl.BlockSpec(memory_space=pltpu.HBM),
+        scratch_shapes=[
+            pltpu.VMEM((height, depth), BF),
+            pltpu.VMEM((width // block, height, block), BF),
+            pltpu.SemaphoreType.DMA((width // block,)),
+        ],
+        compiler_params=pltpu.CompilerParams(vmem_limit_bytes=32 * 2**20),
         name="project",
     )(lhs, weight)
 

time: 42.7 us -> 37.9 us (0.89)
  Pallas kernels: 42.5 us -> 37.8 us
    pallas_call x1, Pallas kernels: 9.34 us -> 4.97 us  [project(): pl.pallas_call(project_kernel, out_shape=jax.ShapeDtypeStruct((height, wi...]
where the time goes in v5:
time: 37.9 us; the launch traced here: 37.8 us
  Pallas kernels  37.8 us (100%)
    pallas_call x1, Pallas kernels, regroup(): pl.pallas_call(functools.partial(kernel, n, nz, parts), out_shape=(jax.Sh...  32.8 us
    pallas_call x1, Pallas kernels, project(): pl.pallas_call(project_kernel, out_shape=jax.ShapeDtypeStruct((height, wi...  4.97 us

profile of v5, /device:TPU:0, one launch (start us, length us, event | category | flops | bytes accessed | tf_op | source)
XLA Modules:
  0.0 37.8 jit_solution(16899536356649146703)
XLA Ops:
  0.0 32.8 %convolve_and_regroup.1 = (bf16[256,1024]{1,0:T(8,128)(2,1)S(1)}, bf16[256,4096]{1,0:T(8,128)(2,1)S(1)}) custom-call(bf16[64,4096]{1,0:T(8,128)(2,1)} %refs_0_.1, bf16[64,4096]{1,0:T(8,128)(2,1)} %refs_1_.1, f32[64,4096]{1,0:T(8,128)} %refs_2_.1, bf16[64,4096]{1,0:T(8,128)(2,1)} %refs_3_.1, f32[64]{0:T(128)} %refs_4_.1, f32[512,256]{1,0:T(8,128)} %constant.12.clone.refs_5_, ...), custom_call_target="tpu_custom_call" | custom-call | tf_op jit(solution)/shard_map/convolve_and_regroup/pallas_call | solution.py:243
  32.8 5.0 %project.1 = bf16[1024,4096]{1,0:T(8,128)(2,1)} custom-call(bf16[256,1024]{1,0:T(8,128)(2,1)S(1)} %get-tuple-element.7.lhs, bf16[256,4096]{1,0:T(8,128)(2,1)S(1)} %get-tuple-element.8.weight), custom_call_target="tpu_custom_call" | custom-call | tf_op jit(solution)/shard_map/project/pallas_call | solution.py:303

commit v6 on v5

--- a/solution.py
+++ b/solution.py
@@ -217,9 +217,10 @@
         out_copies.append(send_out(q))
         if q + 3 < parts:
             in_copies.append(send_in(q + 3))
-        if q >= 1:
-            z_copies.append(send_z(q - 1))
-    z_copies.append(send_z(parts - 1))
+        if q >= 2:
+            z_copies.append(send_z(q - 2))
+    for q in range(max(0, parts - 2), parts):
+        z_copies.append(send_z(q))
     for q in range(parts):
         finish(q)
     for copies in in_copies + out_copies + z_copies:

time: 37.9 us -> 38.8 us (1.024)
  Pallas kernels: 37.8 us -> 38.7 us
    pallas_call x1, Pallas kernels: 32.8 us -> 33.7 us  [regroup(): pl.pallas_call(functools.partial(kernel, n, nz, parts), out_shape=(jax.Sh...]
where the time goes in v6:
time: 38.8 us; the launch traced here: 38.7 us
  Pallas kernels  38.7 us (100%)
    pallas_call x1, Pallas kernels, regroup(): pl.pallas_call(functools.partial(kernel, n, nz, parts), out_shape=(jax.Sh...  33.7 us
    pallas_call x1, Pallas kernels, project(): pl.pallas_call(project_kernel, out_shape=jax.ShapeDtypeStruct((height, wi...  4.97 us

profile of v6, /device:TPU:0, one launch (start us, length us, event | category | flops | bytes accessed | tf_op | source)
XLA Modules:
  0.0 38.7 jit_solution(16825969565339481338)
XLA Ops:
  0.0 33.7 %convolve_and_regroup.1 = (bf16[256,1024]{1,0:T(8,128)(2,1)S(1)}, bf16[256,4096]{1,0:T(8,128)(2,1)S(1)}) custom-call(bf16[64,4096]{1,0:T(8,128)(2,1)} %refs_0_.1, bf16[64,4096]{1,0:T(8,128)(2,1)} %refs_1_.1, f32[64,4096]{1,0:T(8,128)} %refs_2_.1, bf16[64,4096]{1,0:T(8,128)(2,1)} %refs_3_.1, f32[64]{0:T(128)} %refs_4_.1, f32[512,256]{1,0:T(8,128)} %constant.12.clone.refs_5_, ...), custom_call_target="tpu_custom_call" | custom-call | tf_op jit(solution)/shard_map/convolve_and_regroup/pallas_call | solution.py:244
  33.7 5.0 %project.1 = bf16[1024,4096]{1,0:T(8,128)(2,1)} custom-call(bf16[256,1024]{1,0:T(8,128)(2,1)S(1)} %get-tuple-element.7.lhs, bf16[256,4096]{1,0:T(8,128)(2,1)S(1)} %get-tuple-element.8.weight), custom_call_target="tpu_custom_call" | custom-call | tf_op jit(solution)/shard_map/project/pallas_call | solution.py:304

commit v7 on v5

--- a/solution.py
+++ b/solution.py
@@ -215,8 +215,8 @@
         narrow[...] = wide[...].astype(BF)
     for q in range(parts):
         out_copies.append(send_out(q))
-        if q + 3 < parts:
-            in_copies.append(send_in(q + 3))
+        if q >= 1 and q + 2 < parts:
+            in_copies.append(send_in(q + 2))
         if q >= 1:
             z_copies.append(send_z(q - 1))
     z_copies.append(send_z(parts - 1))

time: 37.9 us -> 37.6 us (level)
  no operation moved by 1% of the time
where the time goes in v7:
time: 37.6 us; the launch traced here: 37.5 us
  Pallas kernels  37.5 us (100%)
    pallas_call x1, Pallas kernels, regroup(): pl.pallas_call(functools.partial(kernel, n, nz, parts), out_shape=(jax.Sh...  32.5 us
    pallas_call x1, Pallas kernels, project(): pl.pallas_call(project_kernel, out_shape=jax.ShapeDtypeStruct((height, wi...  4.97 us

profile of v7, /device:TPU:0, one launch (start us, length us, event | category | flops | bytes accessed | tf_op | source)
XLA Modules:
  0.0 37.5 jit_solution(13049736780499650264)
XLA Ops:
  0.0 32.5 %convolve_and_regroup.1 = (bf16[256,1024]{1,0:T(8,128)(2,1)S(1)}, bf16[256,4096]{1,0:T(8,128)(2,1)S(1)}) custom-call(bf16[64,4096]{1,0:T(8,128)(2,1)} %refs_0_.1, bf16[64,4096]{1,0:T(8,128)(2,1)} %refs_1_.1, f32[64,4096]{1,0:T(8,128)} %refs_2_.1, bf16[64,4096]{1,0:T(8,128)(2,1)} %refs_3_.1, f32[64]{0:T(128)} %refs_4_.1, f32[512,256]{1,0:T(8,128)} %constant.12.clone.refs_5_, ...), custom_call_target="tpu_custom_call" | custom-call | tf_op jit(solution)/shard_map/convolve_and_regroup/pallas_call | solution.py:243
  32.5 5.0 %project.1 = bf16[1024,4096]{1,0:T(8,128)(2,1)} custom-call(bf16[256,1024]{1,0:T(8,128)(2,1)S(1)} %get-tuple-element.7.lhs, bf16[256,4096]{1,0:T(8,128)(2,1)S(1)} %get-tuple-element.8.weight), custom_call_target="tpu_custom_call" | custom-call | tf_op jit(solution)/shard_map/project/pallas_call | solution.py:303
